TPU v7x, 256 devices: a whole 4x4x8 slice. The times are simulated.
256 devices in a mesh: region: 32 (over y, x, core), replica: 8 (over z).
Axes of the slice: x: 4, y: 4, z: 8, core: 2. Of those that a mesh axis runs over, the one named last changes fastest.
Arguments:
- positions: float32 [3, 16384, 64], P(None, ('region', 'replica')), may hold values from -1 to 1
- spacing: bfloat16 [16384, 64], P(('region', 'replica')), may hold values from 0.0049743652 to 0.059814453
- targets: float32 [3, 16384], P(None, ('region', 'replica')), may hold values from 0 to 1
- seg_region: int32 [16384, 4, 1], P(('region', 'replica')), may hold values from 0 to 63; in each aligned block of 256 rows (0 to 255, 256 to 511, ..., all dimensions but the last counted through in order) at most 12 rows name the same one
- seg_rank: int32 [16384, 4], P(('region', 'replica')), may hold values from 0 to 3, each once within a row
- frequencies: float32 [3, 128], replicated, may hold values from -6 to 6
- w_in: float32 [64, 256, 256], P('region'), may hold values from -0.375 to 0.375
- w_mid: float32 [64, 256, 256], P('region'), may hold values from -0.375 to 0.375
- w_out: float32 [64, 4, 256], P('region'), may hold values from -0.375 to 0.375
Outputs:
- colour: float32 [3, 16384], P(None, ('region', 'replica'))
- grad_in: float32 [64, 256, 256], P('region')
- grad_mid: float32 [64, 256, 256], P('region')
- grad_out: float32 [64, 4, 256], P('region')
Inputs may be any that keep to these rules, and one draw needn't show every extreme that they name: `seg_region`: among the 256 segments of the rays of one device no region is named more than 12 times. `seg_rank`: each ray's row is a permutation.
All inputs are finite; a program needn't handle non-finite values.
Results may differ from a plain program's by a relative error of at most 0.014.
The roundings to bfloat16 on the way count: a program that leaves them out, or rounds other values in their place, can miss the bound.
Values may be sent and summed in bfloat16 or wider, within the bound.
A program may use at most 128 MiB of HBM per device.

v0:
```python
import functools

import jax
import jax.numpy as jnp
from jax import lax
from jax.experimental import pallas as pl
from jax.experimental.pallas import tpu as pltpu
from jax.sharding import PartitionSpec as P

MESH = pl.DeviceIdType.MESH
f32, bf16 = jnp.float32, jnp.bfloat16
LANES = 128
ROW = 16
loss_scale = 16.0

SIN_HALF = (4.442882919048677, -7.308245676836255, 3.606354025126868, -0.8461104138552027, 0.10982204430121903)
COS_HALF = (1.4142134959439656, -6.978850908781684, 5.739459581977078, -1.8835528214703008, 0.31067786282805515)


def iota(shape, dim):
    return lax.broadcasted_iota(jnp.int32, shape, dim)


def dot(a, b):
    return jnp.dot(a, b, preferred_element_type=f32)


def dot_nt(a, b):
    return lax.dot_general(a, b, (((1,), (1,)), ((), ())), preferred_element_type=f32)


def dot_tn(a, b):
    return lax.dot_general(a, b, (((0,), (0,)), ((), ())), preferred_element_type=f32)


def split(x):
    high = x.astype(bf16).astype(f32)
    rest = x - high
    middle = rest.astype(bf16).astype(f32)
    return high, middle, rest - middle


def wide(x):
    return jnp.concatenate(split(x), 1).astype(bf16)


def tall(x):
    return jnp.concatenate((*split(x), jnp.zeros_like(x)), 0).astype(bf16)


def unwide(x):
    w = x.shape[1] // 3
    return x[:, :w] + x[:, w : 2 * w] + x[:, 2 * w :]


def untall(x):
    w = x.shape[0] // 4
    return x[:w] + x[w : 2 * w] + x[2 * w : 3 * w]


def polynomial(coefficients, z):
    value = jnp.full_like(z, coefficients[-1])
    for coefficient in coefficients[-2::-1]:
        value = value * z + coefficient
    return value


def sin_cos_turns(turns):
    rest = turns - jnp.round(turns)
    square = rest * rest
    s = polynomial(SIN_HALF, square) * rest
    c = polynomial(COS_HALF, square)
    return s * c, 1.0 - s * s


def column_from_row(eye, row):
    return jnp.sum(jnp.where(eye, jnp.broadcast_to(row, eye.shape), 0.0), axis=1, keepdims=True)


def on_lanes(x, width=LANES):
    return jnp.concatenate([x, jnp.zeros((x.shape[0], width - x.shape[1]), x.dtype)], 1)


def exchange_start(count, me, axis, source_of, target, send, recv):
    def start(k, carry):
        peer = lax.rem(me + k, count)
        pltpu.make_async_remote_copy(
            src_ref=source_of(peer),
            dst_ref=target.at[me],
            send_sem=send.at[k],
            recv_sem=recv.at[k],
            device_id={axis: peer},
            device_id_type=MESH,
        ).start()
        return carry

    lax.fori_loop(1, count, start, 0)


def exchange_wait(count, me, axis, source_of, target, send, recv):
    def wait(k, carry):
        peer = lax.rem(me + k, count)
        origin = lax.rem(me + count - k, count)
        pltpu.make_async_remote_copy(
            src_ref=source_of(peer),
            dst_ref=target.at[origin],
            send_sem=send.at[k],
            recv_sem=recv.at[k],
            device_id={axis: peer},
            device_id_type=MESH,
        ).wait()
        return carry

    lax.fori_loop(1, count, wait, 0)


def step_kernel(
    n, m, cap, segs, seg_len,
    pos_ref, gap_ref, tgt_ref, reg_ref, rank_ref, freq_ref, w_out_ref, w_in_hbm, w_mid_hbm,
    colour_ref, grads_ref, grad_out_ref,
    send_a, recv_a, send_b, recv_b, send_c, recv_c,
    feat, hid_one, hid_two, raw, shade, alpha, gaps, raw_grad, grad_two, feat_t, one_t,
    place, phase_hi, phase_lo, slots_x, w_in, w_mid, wb_in, wb_mid, wb_out, wb_out_t,
    acc, acc_out, part, part_recv, out_send, out_recv,
    sem_w, sem_a, sem_b, sem_c, sem_rs, sem_ag, sem_go,
):
    me = lax.axis_index("region")
    mez = lax.axis_index("replica")
    owned = w_in.shape[0]
    rays = pos_ref.shape[1]
    seg_dev = rays * segs
    slots = n * cap
    chunks = seg_len // 2
    per_tile = LANES // ROW
    half_lanes = LANES // 2

    barrier = pltpu.get_barrier_semaphore()

    def greet_region(k, carry):
        pl.semaphore_signal(
            barrier, inc=1, device_id={"region": lax.rem(me + k, n)}, device_id_type=MESH
        )
        return carry

    def greet_replica(k, carry):
        pl.semaphore_signal(
            barrier, inc=1, device_id={"replica": lax.rem(mez + k, m)}, device_id_type=MESH
        )
        return carry

    lax.fori_loop(1, n, greet_region, 0)
    lax.fori_loop(1, m, greet_replica, 0)
    load_in = pltpu.make_async_copy(w_in_hbm, w_in, sem_w.at[0])
    load_mid = pltpu.make_async_copy(w_mid_hbm, w_mid, sem_w.at[1])
    load_in.start()
    load_mid.start()

    eye = iota((rays, rays), 0) == iota((rays, rays), 1)
    region_col = jnp.concatenate([column_from_row(eye, reg_ref[s].astype(f32)) for s in range(segs)], 0)
    lane = iota((seg_dev, LANES), 1)
    onehot = jnp.where(region_col == lane.astype(f32), 1.0, 0.0)
    before = jnp.where(iota((seg_dev, seg_dev), 0) > iota((seg_dev, seg_dev), 1), 1.0, 0.0)
    earlier = dot(before.astype(bf16), onehot.astype(bf16))
    order_col = jnp.sum(earlier * onehot, axis=1, keepdims=True)
    owner_col = jnp.floor((region_col + 0.5) * (1.0 / owned))
    local_col = region_col - owned * owner_col
    keys = jnp.where(lane == 0, owner_col * ROW + order_col, jnp.where(lane == 1, owner_col, 0.0)).T
    slot_row, owner_row = keys[0:1, :], keys[1:2, :]

    pieces = []
    lane_s = iota((rays, LANES), 1) & (half_lanes - 1)
    for s in range(segs):
        packed = jnp.zeros((rays, LANES), f32)
        for d in range(4):
            source = on_lanes(pos_ref[d] if d < 3 else gap_ref[...].astype(f32))
            shift = seg_len * (d - s)
            moved = pltpu.roll(source, shift % LANES, 1)
            packed = jnp.where((lane_s >= seg_len * d) & (lane_s < seg_len * (d + 1)), moved, packed)
        pieces.append(packed[:, :])
    packed = jnp.concatenate(pieces, 0)
    packed = jnp.where(lane < half_lanes, packed, pltpu.roll(packed, half_lanes, 1))
    own_half = (lane >= half_lanes).astype(f32) == local_col
    packed = wide(jnp.where(own_half, packed, 0.0))
    scatter = jnp.where(iota((n * ROW, seg_dev), 0).astype(f32) == slot_row, 1.0, 0.0).astype(bf16)
    send_a[...] = unwide(dot(scatter, packed)).reshape(send_a.shape)

    pl.semaphore_wait(barrier, n - 1 + m - 1)
    exchange_a = (n, me, "region", lambda p: send_a.at[p], recv_a, sem_a.at[0], sem_a.at[1])
    exchange_start(*exchange_a)
    recv_a[me] = send_a[me]

    slot_id = iota((slots, 1), 0).astype(f32)
    peer_id = jnp.floor((slot_id + 0.5) * (1.0 / cap))
    spot = slot_id + (ROW - cap) * peer_id
    place[...] = jnp.where(iota((slots, n * ROW), 1).astype(f32) == spot, 1.0, 0.0).astype(bf16)
    freq_high, freq_middle, freq_low = split(freq_ref[...])
    width = freq_ref.shape[1]

    def spread(values):
        return jnp.concatenate([jnp.broadcast_to(values[d : d + 1], (seg_len, width)) for d in range(3)], 0)

    rest16 = jnp.zeros((seg_len, width), f32)
    rest32 = jnp.zeros((2 * seg_len, width), f32)
    table_hi = jnp.concatenate(
        [spread(freq_high), spread(freq_high), rest32, spread(freq_high), rest16, spread(freq_middle), rest16], 0
    )
    table_lo = jnp.concatenate([spread(freq_low), spread(freq_middle), rest32], 0)
    for i in range(seg_len):
        cols = slice((i % 2) * width, (i % 2 + 1) * width)
        mine = (iota(table_hi.shape, 0) & (seg_len - 1)) == i
        phase_hi[i // 2, :, cols] = jnp.where(mine, table_hi, 0.0).astype(bf16)
        mine = (iota(table_lo.shape, 0) & (seg_len - 1)) == i
        phase_lo[i // 2, :, cols] = jnp.where(mine, table_lo, 0.0).astype(bf16)
    load_in.wait()
    load_mid.wait()
    for l in range(owned):
        wb_in[l] = w_in[l].astype(bf16)
        wb_mid[l] = w_mid[l].astype(bf16)
        out_rows = jnp.concatenate([w_out_ref[l], jnp.zeros((LANES - 4, w_out_ref.shape[2]), f32)], 0)
        wb_out[l] = out_rows[:8].astype(bf16)
        wb_out_t[l] = out_rows.T.astype(bf16)

    exchange_wait(*exchange_a)

    high, middle, low = split(recv_a[...].reshape(n * ROW, LANES))
    lane_r = iota(high.shape, 1)
    coords = 3 * seg_len
    high_turned = pltpu.roll(high, half_lanes, 1)
    pick_gap = jnp.where(
        iota((seg_len, 2 * LANES), 1) == iota((seg_len, 2 * LANES), 0) + LANES + coords, 1.0, 0.0
    ).astype(bf16)
    for l in range(owned):
        own, other = (high, high_turned) if l == 0 else (high_turned, high)
        tail = low if l == 0 else pltpu.roll(low, half_lanes, 1)
        first = jnp.where(lane_r < coords, own, pltpu.roll(middle, coords + l * half_lanes, 1))
        second = jnp.where(lane_r < coords, tail, jnp.where(lane_r < half_lanes, own, other))
        slots_x[l] = dot(place[...], jnp.concatenate([first, second], 1).astype(bf16)).astype(bf16)
        gaps[l] = dot_nt(pick_gap, slots_x[l])

    def phases(l, c):
        return dot(slots_x[l], phase_hi[c]) + dot(slots_x[l][:, :LANES], phase_lo[c])

    def encode(l, c, turns):
        sines, cosines = sin_cos_turns(turns)
        for j in range(2):
            cols = slice(j * width, (j + 1) * width)
            feat[l, c, j * slots : (j + 1) * slots, :] = jnp.concatenate(
                [sines[:, cols], cosines[:, cols]], 1
            ).astype(bf16)

    def render(l):
        depth = jnp.zeros((8, slots), f32)
        clear = jnp.ones((8, slots), f32)
        colour = jnp.zeros((8, slots), f32)
        for i in range(seg_len):
            value = raw[l, i // 2][:, (i % 2) * slots : (i % 2 + 1) * slots]
            density = jnp.broadcast_to(value[0:1], value.shape)
            density = jnp.maximum(density, 0.0) + jnp.log1p(jnp.exp(-jnp.abs(density)))
            emitted = 1.0 / (1.0 + jnp.exp(-value))
            depth = depth + density * gaps[l][i : i + 1]
            after = jnp.exp(-depth)
            colour = colour + (clear - after) * emitted
            clear = after
            shade[l, i] = emitted
            alpha[l, i] = after
        return jnp.where(sub == 0, clear, colour)[:4]

    sub = iota((8, slots), 0)
    steps = [(l, c) for l in range(owned) for c in range(chunks)]
    encode(*steps[0], phases(*steps[0]))
    rendered = []
    for at, (l, c) in enumerate(steps):
        ahead = steps[at + 1] if at + 1 < len(steps) else None
        if ahead:
            turns = phases(*ahead)
        one = jnp.maximum(dot(feat[l, c], wb_in[l]), 0.0).astype(bf16)
        hid_one[l, c] = one
        if ahead:
            encode(*ahead, turns)
        two = jnp.maximum(dot(one, wb_mid[l]), 0.0).astype(bf16)
        hid_two[l, c] = two
        raw[l, c] = dot(two, wb_out_t[l]).T[:8]
        if c == chunks - 1:
            rendered.append(render(l))
    returned = untall(dot(tall(jnp.concatenate(rendered, 0)), place[...]))
    for q in range(send_b.shape[0]):
        send_b[q] = returned[:, q * LANES : (q + 1) * LANES]

    exchange_b = (n, me, "region", lambda p: send_b.at[p // per_tile], recv_b, sem_b.at[0], sem_b.at[1])
    exchange_start(*exchange_b)
    recv_b[me] = send_b[me // per_tile]

    unit_mask = ((lane & (ROW - 1)).astype(f32) == order_col) & own_half
    channel = (lane // ROW) & 3
    owner_mask = jnp.where(iota((seg_dev, n), 1).astype(f32) == owner_col, 1.0, 0.0).astype(bf16)
    owner_turned = jnp.where(iota((n, seg_dev), 0).astype(f32) == owner_row, 1.0, 0.0).astype(bf16)
    rank = [column_from_row(eye, rank_ref[s : s + 1, :].astype(f32)) for s in range(segs)]
    earlier_than = [[rank[t] < rank[s] for t in range(segs)] for s in range(segs)]
    target = [column_from_row(eye, tgt_ref[c : c + 1, :]) for c in range(3)]
    shift_home = lax.rem(me, per_tile) * ROW

    for l in range(owned):
        for c in range(chunks):
            one_t[l, c] = hid_one[l, c].T

    exchange_wait(*exchange_b)

    lane_n = iota((n, LANES), 1)
    mine = jnp.zeros((n, LANES), f32)
    for ch in range(8):
        moved = pltpu.roll(recv_b[:, ch, :], lax.rem(ch * ROW - shift_home + LANES, LANES), 1)
        mine = jnp.where((lane_n >= ch * ROW) & (lane_n < (ch + 1) * ROW), moved, mine)
    found = jnp.where(unit_mask, unwide(dot(owner_mask, wide(mine))), 0.0)
    columns = [jnp.sum(jnp.where(channel == ch, found, 0.0), axis=1, keepdims=True) for ch in range(4)]
    by_seg = [[col[s * rays : (s + 1) * rays] for s in range(segs)] for col in columns]
    trans, colours = by_seg[0], by_seg[1:]

    def front(s, skip):
        product = jnp.ones((rays, 1), f32)
        for t in range(segs):
            if t not in skip:
                product = product * jnp.where(earlier_than[s][t], trans[t], 1.0)
        return product

    prefix = [front(s, (s,)) for s in range(segs)]
    pulled = []
    for c in range(3):
        total = colours[c][0] * prefix[0]
        for s in range(1, segs):
            total = total + colours[c][s] * prefix[s]
        colour_ref[c : c + 1, :] = jnp.sum(
            jnp.where(eye, jnp.broadcast_to(total, eye.shape), 0.0), axis=0, keepdims=True
        )
        pulled.append((2.0 * loss_scale) * (total - target[c]))
    weight = [
        pulled[0] * colours[0][s] + pulled[1] * colours[1][s] + pulled[2] * colours[2][s] for s in range(segs)
    ]
    back = [[], [], [], []]
    for t in range(segs):
        total = jnp.zeros((rays, 1), f32)
        for s in range(segs):
            if s != t:
                total = total + jnp.where(earlier_than[s][t], weight[s] * front(s, (s, t)), 0.0)
        back[0].append(total)
        for c in range(3):
            back[c + 1].append(pulled[c] * prefix[t])
    spread_back = jnp.zeros((seg_dev, LANES), f32)
    for ch in range(4):
        spread_back = jnp.where(channel == ch, jnp.concatenate(back[ch], 0), spread_back)
    spread_back = jnp.where(unit_mask, spread_back, 0.0)
    homeward = unwide(dot(owner_turned, wide(spread_back)))
    for ch in range(8):
        moved = pltpu.roll(homeward, lax.rem(shift_home - ch * ROW + LANES, LANES), 1)
        send_c[:, ch, :] = jnp.where((lane_n >= shift_home) & (lane_n < shift_home + ROW), moved, 0.0)

    exchange_c = (n, me, "region", lambda p: send_c.at[p], recv_c, sem_c.at[0], sem_c.at[1])
    exchange_start(*exchange_c)
    recv_c[me] = send_c[me]
    for l in range(owned):
        for c in range(chunks):
            feat_t[l, c] = feat[l, c].T
    exchange_wait(*exchange_c)

    groups = []
    for q in range(send_b.shape[0]):
        total = recv_c[q * per_tile]
        for k in range(1, per_tile):
            total = total + recv_c[q * per_tile + k]
        groups.append(total)
    cotangent = untall(dot_nt(tall(jnp.concatenate(groups, 1)), place[...]))

    def render_back(l):
        pull = cotangent if l == 0 else pltpu.roll(cotangent, 4, 0)
        later = pull[0:1] * alpha[l, seg_len - 1][0:1]
        for i in range(seg_len - 1, -1, -1):
            emitted = shade[l, i]
            after = alpha[l, i]
            ahead = alpha[l, i - 1] if i > 0 else jnp.ones_like(after)
            share = ahead - after
            lit = pull * emitted
            lit = jnp.sum(jnp.where((sub >= 1) & (sub <= 3), lit, 0.0), axis=0, keepdims=True)
            later = later + lit * share[0:1]
            density = (lit * ahead[0:1] - later) * gaps[l][i : i + 1] * emitted[0:1]
            tint = pull * share * emitted * (1.0 - emitted)
            values = jnp.where(sub == 0, density, jnp.where(sub <= 3, tint, 0.0))
            raw_grad[l, i // 2, :, (i % 2) * slots : (i % 2 + 1) * slots] = tall(values)

    def exchange_r(p):
        return (m, mez, "replica", lambda z: part.at[p, z], part_recv.at[p], sem_rs.at[p, 0], sem_rs.at[p, 1])

    def exchange_g(p):
        return (m, mez, "replica", lambda z: grads_ref.at[p, mez], grads_ref.at[p], sem_ag.at[p, 0], sem_ag.at[p, 1])

    def send_part(p):
        part[p] = acc[...].astype(bf16).reshape(part.shape[1:])
        exchange_start(*exchange_r(p))

    def sum_part(p):
        part_recv[p, mez] = part[p, mez]
        exchange_wait(*exchange_r(p))
        total = part_recv[p, 0].astype(f32)
        for k in range(1, m):
            total = total + part_recv[p, k].astype(f32)
        grads_ref[p, mez] = total.astype(bf16)

    two_steps = m == 8
    last = 2 * owned - 1

    def hop(p, k, chunk, target):
        return pltpu.make_async_remote_copy(
            src_ref=grads_ref.at[p, chunk],
            dst_ref=grads_ref.at[p, chunk],
            send_sem=sem_ag.at[p, 0, k],
            recv_sem=sem_ag.at[p, 1, k],
            device_id={"replica": target},
            device_id_type=MESH,
        )

    def away(distance):
        return lax.rem(mez + distance + m, m)

    side = 2 - 4 * lax.rem(mez, 2)
    near = ((0, 1), (1, -1), (2, 2), (3, -2))
    far = ((4, away(-2), away(1)), (5, away(2), away(-1)), (6, away(-side), away(side)))

    def gather_near(p):
        if p == last or not two_steps:
            exchange_start(*exchange_g(p))
            return
        for k, distance in near:
            hop(p, k, mez, away(distance)).start()

    def gather_far(p):
        if p == last or not two_steps:
            return
        for k, distance in near[2:]:
            hop(p, k, away(-distance), away(distance)).wait_recv()
        for k, chunk, target in far:
            hop(p, k, chunk, target).start()

    def gather_wait(p):
        if p == last or not two_steps:
            exchange_wait(*exchange_g(p))
            return
        for k, distance in near[:2]:
            hop(p, k, away(-distance), away(distance)).wait_recv()
        for k, distance in ((4, -3), (5, 3), (6, 4)):
            hop(p, k, away(distance), away(1)).wait_recv()
        for k, distance in near:
            hop(p, k, mez, away(distance)).wait_send()
        for k, chunk, target in far:
            hop(p, k, chunk, target).wait_send()

    for l in range(owned):
        render_back(l)
    for l in range(owned):
        head = jnp.concatenate([wb_out[l].astype(f32)] * 4, 0).astype(bf16)

        def second_grad(c):
            grad_two[l, c] = jnp.where(hid_two[l, c] > 0, dot_tn(raw_grad[l, c], head), 0.0).astype(bf16)

        def first_grad(c):
            return jnp.where(hid_one[l, c] > 0, dot_nt(grad_two[l, c], wb_mid[l]), 0.0).astype(bf16)

        second_grad(0)
        for c in range(chunks):
            if c + 1 < chunks:
                second_grad(c + 1)
            term = dot(one_t[l, c], grad_two[l, c])
            acc[...] = term if c == 0 else acc[...] + term
            term = dot(raw_grad[l, c], hid_two[l, c])
            acc_out[...] = term if c == 0 else acc_out[...] + term
        send_part(2 * l)
        summed = untall(acc_out[...])[:4]
        half = summed.shape[1] // 2
        out_send[l] = jnp.concatenate([summed[:, :half], summed[:, half:]], 0)
        if l > 0:
            sum_part(2 * l - 2)
            gather_near(2 * l - 2)
        now = first_grad(0)
        for c in range(chunks):
            later = first_grad(c + 1) if c + 1 < chunks else None
            term = dot(feat_t[l, c], now)
            acc[...] = term if c == 0 else acc[...] + term
            now = later
        send_part(2 * l + 1)

    exchange_o = (m, mez, "replica", lambda z: out_send, out_recv, sem_go.at[0], sem_go.at[1])
    exchange_start(*exchange_o)
    out_recv[mez] = out_send[...]
    for p in range(last - 2, last):
        sum_part(p)
        gather_near(p)
        gather_far(p - 1)
    gather_far(last - 1)
    sum_part(last)
    gather_near(last)
    exchange_wait(*exchange_o)
    total = out_recv[0]
    for k in range(1, m):
        total = total + out_recv[k]
    for l in range(owned):
        grad_out_ref[l] = jnp.concatenate([total[l, :4], total[l, 4:]], 1)
    for p in range(2 * owned):
        gather_wait(p)


def finish_kernel(colour, grads, grad_out, colour_ref, grad_in_ref, grad_mid_ref, grad_out_ref):
    colour_ref[...] = colour[...]
    grad_out_ref[...] = grad_out[...]
    for l in range(grad_in_ref.shape[0]):
        grad_mid_ref[l] = grads[2 * l].astype(f32)
        grad_in_ref[l] = grads[2 * l + 1].astype(f32)


def on_device(positions, spacing, targets, seg_region, seg_rank, frequencies, w_in, w_mid, w_out):
    n, m = lax.axis_size("region"), lax.axis_size("replica")
    rays, segs = seg_rank.shape
    seg_len = positions.shape[2] // segs
    owned, enc, hid = w_in.shape
    cap = 3 * rays * segs // (owned * n)
    slots, chunk = n * cap, 2 * n * cap
    chunks = seg_len // 2
    groups = n * ROW // LANES
    deep = hid // m
    half = w_out.shape[2] // 2
    vmem = pltpu.VMEM
    semaphores = pltpu.SemaphoreType.DMA
    colour, grads, grad_out = pl.pallas_call(
        functools.partial(step_kernel, n, m, cap, segs, seg_len),
        out_shape=(
            jax.ShapeDtypeStruct((3, rays), f32),
            jax.ShapeDtypeStruct((2 * owned, m, deep, hid), bf16),
            jax.ShapeDtypeStruct(w_out.shape, f32),
        ),
        in_specs=[pl.BlockSpec(memory_space=vmem)] * 7 + [pl.BlockSpec(memory_space=pl.ANY)] * 2,
        out_specs=[pl.BlockSpec(memory_space=vmem)] * 3,
        scratch_shapes=[
            vmem((n, ROW, LANES), f32),
            vmem((n, ROW, LANES), f32),
            vmem((groups, 8, LANES), f32),
            vmem((n, 8, LANES), f32),
            vmem((n, 8, LANES), f32),
            vmem((n, 8, LANES), f32),
            vmem((owned, chunks, chunk, enc), bf16),
            vmem((owned, chunks, chunk, hid), bf16),
            vmem((owned, chunks, chunk, hid), bf16),
            vmem((owned, chunks, 8, chunk), f32),
            vmem((owned, seg_len, 8, slots), f32),
            vmem((owned, seg_len, 8, slots), f32),
            vmem((owned, seg_len, slots), f32),
            vmem((owned, chunks, 32, chunk), bf16),
            vmem((owned, chunks, chunk, hid), bf16),
            vmem((owned, chunks, enc, chunk), bf16),
            vmem((owned, chunks, hid, chunk), bf16),
            vmem((slots, n * ROW), bf16),
            vmem((chunks, 2 * LANES, enc), bf16),
            vmem((chunks, LANES, enc), bf16),
            vmem((owned, slots, 2 * LANES), bf16),
            vmem((owned, enc, hid), f32),
            vmem((owned, hid, hid), f32),
            vmem((owned, enc, hid), bf16),
            vmem((owned, hid, hid), bf16),
            vmem((owned, 8, hid), bf16),
            vmem((owned, hid, LANES), bf16),
            vmem((hid, hid), f32),
            vmem((32, hid), f32),
            vmem((2 * owned, m, deep, hid), bf16),
            vmem((2 * owned, m, deep, hid), bf16),
            vmem((owned, 8, half), f32),
            vmem((m, owned, 8, half), f32),
            semaphores((2,)),
            semaphores((2, n)),
            semaphores((2, n)),
            semaphores((2, n)),
            semaphores((2 * owned, 2, m)),
            semaphores((2 * owned, 2, m)),
            semaphores((2, m)),
        ],
        compiler_params=pltpu.CompilerParams(
            collective_id=0, has_side_effects=True, vmem_limit_bytes=56 * 2**20
        ),
        name="radiance_step",
    )(
        positions, spacing, targets, seg_region.transpose(1, 2, 0), seg_rank.T, frequencies, w_out, w_in, w_mid
    )
    return pl.pallas_call(
        finish_kernel,
        out_shape=(
            jax.ShapeDtypeStruct(colour.shape, f32),
            jax.ShapeDtypeStruct(w_in.shape, f32),
            jax.ShapeDtypeStruct(w_mid.shape, f32),
            jax.ShapeDtypeStruct(w_out.shape, f32),
        ),
        in_specs=[pl.BlockSpec(memory_space=vmem)] * 3,
        out_specs=[pl.BlockSpec(memory_space=vmem)] * 4,
        name="widen",
    )(colour, grads.reshape(2 * owned, hid, hid), grad_out)


def solution(mesh):
    in_specs = (
        P(None, ("region", "replica"), None),
        P(("region", "replica"), None),
        P(None, ("region", "replica")),
        P(("region", "replica"), None, None),
        P(("region", "replica"), None),
        P(),
        P("region", None, None),
        P("region", None, None),
        P("region", None, None),
    )
    out_specs = (
        P(None, ("region", "replica")),
        P("region", None, None),
        P("region", None, None),
        P("region", None, None),
    )
    return jax.shard_map(
        on_device, mesh=mesh, in_specs=in_specs, out_specs=out_specs, check_vma=False
    )
```

profile of v0, /device:TPU:2, one launch (start us, length us, event | category | flops | bytes accessed | tf_op | source)
XLA Modules:
  0.0 74.3 jit_solution(7369754240567550163)
XLA Ops:
  0.6 71.6 %radiance_step.1 = (f32[3,64]{1,0:T(4,128)}, bf16[4,8,32,256]{3,2,1,0:T(8,128)(2,1)}, f32[2,4,256]{2,1,0:T(4,128)}) custom-call(f32[3,64,64]{2,1,0:T(8,128)} %pos_ref.1, bf16[64,64]{1,0:T(8,128)(2,1)} %gap_ref.1, f32[3,64]{1,0:T(4,128)} %tgt_ref.1, s32[4,1,64]{2,1,0:T(1,128)} %bitcast.4, s32[4,64]{1,0:T(4,128)} %bitcast.5, f32[3,128]{1,0:T(4,128)} %freq_ref.1, ...), custom_call_target="tpu_custom_call" | custom-call | tf_op jit(solution)/shard_map/radiance_step/pallas_call | solution.py:529
  72.3 2.0 %widen.1 = (f32[3,64]{1,0:T(4,128)}, f32[2,256,256]{2,1,0:T(8,128)}, f32[2,256,256]{2,1,0:T(8,128)}, f32[2,4,256]{2,1,0:T(4,128)}) custom-call(f32[3,64]{1,0:T(4,128)} %get-tuple-element.7.colour, bf16[4,256,256]{2,1,0:T(8,128)(2,1)} %bitcast.3, f32[2,4,256]{2,1,0:T(4,128)} %get-tuple-element.9.grad_out), custom_call_target="tpu_custom_call" | custom-call | tf_op jit(solution)/shard_map/widen/pallas_call | solution.py:587
where the time goes:
time: 75.2 us; the launch traced here: 74.3 us
  Pallas kernels  73.7 us (98%)
    pallas_call x1, Pallas kernels, on_device(): pl.pallas_call(functools.partial(step_kernel, n, m, cap, segs, seg_len),...  71.6 us
    pallas_call x1, Pallas kernels, on_device(): pl.pallas_call(finish_kernel, out_shape=(jax.ShapeDtypeStruct(colour.shap...  2.05 us

commit v1 on v0

--- a/solution.py
+++ b/solution.py
@@ -97,18 +97,22 @@
     lax.fori_loop(1, count, start, 0)
 
 
-def exchange_wait(count, me, axis, source_of, target, send, recv):
+def exchange_wait(count, me, axis, source_of, target, send, recv, sides=("recv", "send")):
     def wait(k, carry):
         peer = lax.rem(me + k, count)
         origin = lax.rem(me + count - k, count)
-        pltpu.make_async_remote_copy(
+        copy = pltpu.make_async_remote_copy(
             src_ref=source_of(peer),
             dst_ref=target.at[origin],
             send_sem=send.at[k],
             recv_sem=recv.at[k],
             device_id={axis: peer},
             device_id_type=MESH,
-        ).wait()
+        )
+        if "recv" in sides:
+            copy.wait_recv()
+        if "send" in sides:
+            copy.wait_send()
         return carry
 
     lax.fori_loop(1, count, wait, 0)
@@ -220,7 +224,7 @@
         wb_out[l] = out_rows[:8].astype(bf16)
         wb_out_t[l] = out_rows.T.astype(bf16)
 
-    exchange_wait(*exchange_a)
+    exchange_wait(*exchange_a, ("recv",))
 
     high, middle, low = split(recv_a[...].reshape(n * ROW, LANES))
     lane_r = iota(high.shape, 1)
@@ -266,7 +270,7 @@
         return jnp.where(sub == 0, clear, colour)[:4]
 
     sub = iota((8, slots), 0)
-    steps = [(l, c) for l in range(owned) for c in range(chunks)]
+    steps = [(l, c) for c in range(chunks) for l in range(owned)]
     encode(*steps[0], phases(*steps[0]))
     rendered = []
     for at, (l, c) in enumerate(steps):
@@ -303,7 +307,7 @@
         for c in range(chunks):
             one_t[l, c] = hid_one[l, c].T
 
-    exchange_wait(*exchange_b)
+    exchange_wait(*exchange_b, ("recv",))
 
     lane_n = iota((n, LANES), 1)
     mine = jnp.zeros((n, LANES), f32)
@@ -359,7 +363,7 @@
     for l in range(owned):
         for c in range(chunks):
             feat_t[l, c] = feat[l, c].T
-    exchange_wait(*exchange_c)
+    exchange_wait(*exchange_c, ("recv",))
 
     groups = []
     for q in range(send_b.shape[0]):
@@ -453,7 +457,6 @@
 
     for l in range(owned):
         render_back(l)
-    for l in range(owned):
         head = jnp.concatenate([wb_out[l].astype(f32)] * 4, 0).astype(bf16)
 
         def second_grad(c):
@@ -468,12 +471,7 @@
                 second_grad(c + 1)
             term = dot(one_t[l, c], grad_two[l, c])
             acc[...] = term if c == 0 else acc[...] + term
-            term = dot(raw_grad[l, c], hid_two[l, c])
-            acc_out[...] = term if c == 0 else acc_out[...] + term
         send_part(2 * l)
-        summed = untall(acc_out[...])[:4]
-        half = summed.shape[1] // 2
-        out_send[l] = jnp.concatenate([summed[:, :half], summed[:, half:]], 0)
         if l > 0:
             sum_part(2 * l - 2)
             gather_near(2 * l - 2)
@@ -485,22 +483,37 @@
             now = later
         send_part(2 * l + 1)
 
+    sum_part(1)
+    gather_near(1)
+
+    half = hid_two.shape[3] // 2
+    sums = []
+    for l in range(owned):
+        for c in range(chunks):
+            term = dot(raw_grad[l, c], hid_two[l, c])
+            acc_out[...] = term if c == 0 else acc_out[...] + term
+        summed = untall(acc_out[...])[:4]
+        sums += [summed[:, :half], summed[:, half:]]
+    out_send[...] = jnp.concatenate(sums, 0).astype(bf16)
     exchange_o = (m, mez, "replica", lambda z: out_send, out_recv, sem_go.at[0], sem_go.at[1])
     exchange_start(*exchange_o)
     out_recv[mez] = out_send[...]
-    for p in range(last - 2, last):
-        sum_part(p)
-        gather_near(p)
-        gather_far(p - 1)
-    gather_far(last - 1)
+
+    sum_part(2)
+    gather_near(2)
+    gather_far(0)
+    gather_far(1)
     sum_part(last)
     gather_near(last)
+    gather_far(2)
+    for exchange in (exchange_a, exchange_b, exchange_c):
+        exchange_wait(*exchange, ("send",))
     exchange_wait(*exchange_o)
-    total = out_recv[0]
+    total = out_recv[0].astype(f32)
     for k in range(1, m):
-        total = total + out_recv[k]
+        total = total + out_recv[k].astype(f32)
     for l in range(owned):
-        grad_out_ref[l] = jnp.concatenate([total[l, :4], total[l, 4:]], 1)
+        grad_out_ref[l] = jnp.concatenate([total[8 * l : 8 * l + 4], total[8 * l + 4 : 8 * l + 8]], 1)
     for p in range(2 * owned):
         gather_wait(p)
 
@@ -567,8 +580,8 @@
             vmem((32, hid), f32),
             vmem((2 * owned, m, deep, hid), bf16),
             vmem((2 * owned, m, deep, hid), bf16),
-            vmem((owned, 8, half), f32),
-            vmem((m, owned, 8, half), f32),
+            vmem((8 * owned, half), bf16),
+            vmem((m, 8 * owned, half), bf16),
             semaphores((2,)),
             semaphores((2, n)),
             semaphores((2, n)),

time: 75.2 us -> 73.3 us (0.975)
  Pallas kernels: 73.7 us -> 71.3 us
    pallas_call x1, Pallas kernels: 71.6 us -> 69.3 us  [on_device(): pl.pallas_call(functools.partial(step_kernel, n, m, cap, segs, seg_len),...]
where the time goes in v1:
time: 73.3 us; the launch traced here: 72 us
  Pallas kernels  71.3 us (97%)
    pallas_call x1, Pallas kernels, on_device(): pl.pallas_call(functools.partial(step_kernel, n, m, cap, segs, seg_len),...  69.3 us
    pallas_call x1, Pallas kernels, on_device(): pl.pallas_call(finish_kernel, out_shape=(jax.ShapeDtypeStruct(colour.shap...  2.05 us

profile of v1, /device:TPU:2, one launch (start us, length us, event | category | flops | bytes accessed | tf_op | source)
XLA Modules:
  0.0 72.0 jit_solution(3048590227157456947)
XLA Ops:
  0.6 69.3 %radiance_step.1 = (f32[3,64]{1,0:T(4,128)}, bf16[4,8,32,256]{3,2,1,0:T(8,128)(2,1)}, f32[2,4,256]{2,1,0:T(4,128)}) custom-call(f32[3,64,64]{2,1,0:T(8,128)} %pos_ref.1, bf16[64,64]{1,0:T(8,128)(2,1)} %gap_ref.1, f32[3,64]{1,0:T(4,128)} %tgt_ref.1, s32[4,1,64]{2,1,0:T(1,128)} %bitcast.4, s32[4,64]{1,0:T(4,128)} %bitcast.5, f32[3,128]{1,0:T(4,128)} %freq_ref.1, ...), custom_call_target="tpu_custom_call" | custom-call | tf_op jit(solution)/shard_map/radiance_step/pallas_call | solution.py:542
  69.9 2.0 %widen.1 = (f32[3,64]{1,0:T(4,128)}, f32[2,256,256]{2,1,0:T(8,128)}, f32[2,256,256]{2,1,0:T(8,128)}, f32[2,4,256]{2,1,0:T(4,128)}) custom-call(f32[3,64]{1,0:T(4,128)} %get-tuple-element.7.colour, bf16[4,256,256]{2,1,0:T(8,128)(2,1)} %bitcast.3, f32[2,4,256]{2,1,0:T(4,128)} %get-tuple-element.9.grad_out), custom_call_target="tpu_custom_call" | custom-call | tf_op jit(solution)/shard_map/widen/pallas_call | solution.py:600
